TPU v7x, 128 devices: a whole 4x4x4 slice. The times are simulated.
128 devices in a mesh: inst: 4 (over x_hi, core), seq: 32 (over y, z, x_lo).
Axes of the slice: x: 4 (x_hi: 2, x_lo: 2; x = x_hi * 2 + x_lo), y: 4, z: 4, core: 2. Of those that a mesh axis runs over, the one named last changes fastest.
Arguments:
- query_rows: bfloat16 [16384, 8192], P(('inst', 'seq')), may hold values from -25 to 25
- key_rows: bfloat16 [16384, 1024], P(('inst', 'seq')), may hold values from -4 to 4
- value_rows: bfloat16 [16384, 1024], P(('inst', 'seq')), may hold values from -6 to 6
- target_instance: int32 [8192], P(('inst', 'seq')), may hold values from 0 to 3, as said below
- block_position: int32 [8192], P(('inst', 'seq')), may hold values from 0 to 2047, as said below
- request_lengths: int32 [4, 2], replicated, may hold values from 1 to 3584, 4096 in all within a row
Outputs:
- attended: bfloat16 [16384, 8192], P(('inst', 'seq'))
Inputs may be any that keep to these rules, and one draw needn't show every extreme that they name: `target_instance`: together with block_position, every pair of an instance and a position block is named by exactly one entry block. Of the 64 blocks of one entry device, at most 1 name one instance and block positions b (values of block_position) with the same b // 64, and at most 1 name one instance and block positions with the same min(h, 63 - h), where h = b // 32; both bounds are reached. `block_position`: see target_instance.
All inputs are finite; a program needn't handle non-finite values.
Results may differ from a plain program's by a relative error of at most 0.0055.
Values may be sent and summed in bfloat16 or wider, within the bound.
No kernel may reach another device: no remote copies, remote signals or barrier semaphores. Data moves between devices by JAX's collectives and lax.ppermute only.
A program may use at most 128 MiB of HBM per device.

v0:
```python
import math
import jax
import jax.numpy as jnp
from jax import lax
from jax.sharding import PartitionSpec as P

QUERY_HEADS = 64
KEY_HEADS = 8
HEAD_SIZE = 128


def layout_position(global_rows, row_count, block_rows, half_blocks):
    shard_of = global_rows // row_count
    local_rows = global_rows % row_count
    local_block = local_rows // block_rows
    within = local_rows % block_rows
    offset = local_block % half_blocks
    upper = local_block // half_blocks
    halves = 2 * shard_of + upper
    return (halves * half_blocks + offset) * block_rows + within


def shards(query_rows, key_rows, value_rows, target_instance, block_position, request_lengths):
    inst_count = lax.axis_size("inst")
    seq_count = lax.axis_size("seq")
    devices = inst_count * seq_count
    blocks = block_position.shape[0]
    row_count = query_rows.shape[0]
    block_rows = row_count // blocks
    half_blocks = blocks // 2
    capacity = blocks // (2 * seq_count)
    groups = QUERY_HEADS // KEY_HEADS
    query_width = query_rows.shape[1]
    key_width = key_rows.shape[1]
    score_scale = 1.0 / math.sqrt(HEAD_SIZE)
    own_shard = lax.axis_index("seq")
    instance = lax.axis_index("inst")
    halves = block_position // half_blocks
    offset = block_position % half_blocks
    owner_shard = halves // 2
    local_block = halves % 2 * half_blocks + offset
    target = target_instance * seq_count + owner_shard
    ordinal = jnp.arange(blocks)
    before = (target[:, None] == target[None, :]) & (ordinal[None, :] < ordinal[:, None])
    slot_index = jnp.sum(before.astype(jnp.int32), axis=1)
    destination = target * capacity + slot_index

    def pack_rows(payload, width):
        empty = jnp.zeros((devices * capacity, block_rows, width), payload.dtype)
        filled = empty.at[destination].set(payload.reshape(blocks, block_rows, width))
        return filled.reshape(inst_count, seq_count, capacity, block_rows, width)

    send_query = pack_rows(query_rows, query_width)
    send_key = pack_rows(key_rows, key_width)
    send_value = pack_rows(value_rows, key_width)
    labels = (
        jnp.full((devices * capacity,), -1.0, jnp.bfloat16)
        .at[destination]
        .set(local_block.astype(jnp.bfloat16))
    )
    labels = labels.reshape(inst_count, seq_count, capacity)
    got_query, got_key, got_value, got_label = (
        lax.all_to_all(
            send_query.reshape(devices, capacity, block_rows, query_width),
            ("inst", "seq"),
            split_axis=0,
            concat_axis=0,
            tiled=True,
        ),
        lax.all_to_all(
            send_key.reshape(devices, capacity, block_rows, key_width),
            ("inst", "seq"),
            split_axis=0,
            concat_axis=0,
            tiled=True,
        ),
        lax.all_to_all(
            send_value.reshape(devices, capacity, block_rows, key_width),
            ("inst", "seq"),
            split_axis=0,
            concat_axis=0,
            tiled=True,
        ),
        lax.all_to_all(
            labels.reshape(devices, capacity),
            ("inst", "seq"),
            split_axis=0,
            concat_axis=0,
            tiled=True,
        ),
    )
    received = got_label.reshape(-1).astype(jnp.int32)
    placed = jnp.where(received < 0, blocks, received)

    def unpack_rows(payload, width):
        empty = jnp.zeros((blocks, block_rows, width), payload.dtype)
        filled = empty.at[placed].set(payload.reshape(-1, block_rows, width), mode="drop")
        return filled.reshape(row_count, width)

    local_query = unpack_rows(got_query, query_width)
    local_key = unpack_rows(got_key, key_width)
    local_value = unpack_rows(got_value, key_width)
    lengths_here = lax.dynamic_index_in_dim(request_lengths, instance, 0, keepdims=False)
    request_ends = jnp.cumsum(lengths_here)
    query_pos = layout_position(
        own_shard * row_count + jnp.arange(row_count), row_count, block_rows, half_blocks
    )
    query_start = jnp.sum(
        jnp.where(request_ends[None, :] <= query_pos[:, None], lengths_here[None, :], 0), axis=1
    )
    query_heads = local_query.reshape(row_count, KEY_HEADS, groups, HEAD_SIZE)

    def attend(running, key_block, value_block, key_index):
        key_pos = layout_position(key_index, row_count, block_rows, half_blocks)
        allowed = (key_pos[None, :] <= query_pos[:, None]) & (
            key_pos[None, :] >= query_start[:, None]
        )
        maxima, totals, weighted = running
        key_heads = key_block.reshape(-1, KEY_HEADS, HEAD_SIZE)
        value_heads = value_block.reshape(-1, KEY_HEADS, HEAD_SIZE)
        scores = (
            jnp.einsum("qhgd,khd->hgqk", query_heads, key_heads, preferred_element_type=jnp.float32)
            * score_scale
        )
        masked = jnp.where(allowed, scores, -1e30)
        new_maxima = jnp.maximum(maxima, jnp.max(masked, axis=-1))
        weights = jnp.where(allowed, jnp.exp(scores - new_maxima[..., None]), 0.0)
        rescale = jnp.exp(maxima - new_maxima)
        totals = totals * rescale + jnp.sum(weights, axis=-1)
        weighted = weighted * rescale[..., None] + jnp.einsum(
            "hgqk,khd->hgqd",
            weights.astype(jnp.bfloat16),
            value_heads,
            preferred_element_type=jnp.float32,
        )
        return (new_maxima, totals, weighted)

    initial = (
        jnp.full((KEY_HEADS, groups, row_count), -1e30, jnp.float32),
        jnp.zeros((KEY_HEADS, groups, row_count), jnp.float32),
        jnp.zeros((KEY_HEADS, groups, row_count, HEAD_SIZE), jnp.float32),
    )
    running = initial
    key_piece = lax.all_gather(local_key, "seq", axis=0, tiled=True)
    value_piece = lax.all_gather(local_value, "seq", axis=0, tiled=True)
    piece_rows = key_piece.shape[0]
    shard_count = piece_rows // row_count
    keyed = key_piece.reshape(shard_count, row_count, key_width)
    valued = value_piece.reshape(shard_count, row_count, key_width)
    offsets = jnp.arange(shard_count) * row_count

    def scan_step(state, element):
        key_block, value_block, first_row = element
        return (attend(state, key_block, value_block, first_row + jnp.arange(row_count)), None)

    running, unused = lax.scan(scan_step, running, (keyed, valued, offsets))
    maxima, totals, weighted = running
    attended_local = (
        (weighted / totals[..., None])
        .transpose(2, 0, 1, 3)
        .reshape(row_count, query_width)
        .astype(jnp.bfloat16)
    )
    out_blocks = attended_local.reshape(blocks, block_rows, query_width)
    returning = out_blocks[jnp.clip(received, 0, blocks - 1)]
    returned = lax.all_to_all(
        returning.reshape(devices, capacity, block_rows, query_width),
        ("inst", "seq"),
        split_axis=0,
        concat_axis=0,
        tiled=True,
    )
    gathered_back = returned.reshape(devices * capacity, block_rows, query_width)[destination]
    return gathered_back.reshape(row_count, query_width)


def solution(mesh):
    placed = (
        P(("inst", "seq"), None),
        P(("inst", "seq"), None),
        P(("inst", "seq"), None),
        P(("inst", "seq")),
        P(("inst", "seq")),
        P(),
    )
    return jax.shard_map(
        shards, mesh=mesh, in_specs=placed, out_specs=P(("inst", "seq"), None), check_vma=False
    )
```

profile of v0, /device:TPU:1, one launch (start us, length us, event | category | flops | bytes accessed | tf_op | source)
XLA Modules:
  0.0 1056.4 jit_solution(14671933270696867781)
XLA Ops:
  9.8 11.5 %all-to-all-start = ((bf16[128,1,1]{2,1,0:T(2,128)(2,1)}), bf16[128,1,1]{2,1,0:T(2,128)(2,1)S(1)}, u32[]{:S(2)}, u32[]{:S(2)}) async-start(bf16[128,1,1]{2,1,0:T(2,128)(2,1)} %copy.43), calls=%async_computation | async-start | bytes 131072 | tf_op jit(solution)/shard_map/all_to_all | solution.py:84
  23.5 7.9 scatter_fusion.4
  31.4 9.8 all-to-all-start.3
  43.6 11.3 %all-to-all-done.3 = bf16[128,1,2,1024]{3,2,1,0:T(2,128)(2,1)S(1)} async-done(((bf16[128,1,2,1024]{3,2,1,0:T(2,128)(2,1)}), bf16[128,1,2,1024]{3,2,1,0:T(2,128)(2,1)S(1)}, u32[]{:S(2)}, u32[]{:S(2)}) %all-to-all-start.3) | async-done | bytes 524320 | tf_op jit(solution)/shard_map/all_to_all | solution.py:77
  63.2 23.9 %all_to_all.29 = bf16[128,1,2,1024]{3,2,1,0:T(2,128)(2,1)S(1)} all-to-all(bf16[128,1,2,1024]{3,2,1,0:T(2,128)(2,1)S(1)} %bitcast.80), channel_id=1, replica_groups=mesh['inst'=4,'seq'=32] {'inst','seq'}, dimensions={0} | all-to-all | bytes 1048576 | tf_op jit(solution)/shard_map/all_to_all | solution.py:70
  95.8 6.2 broadcast_in_dim.95
  101.9 14.6 %scatter_fusion.2 = bf16[128,2,8192]{2,1,0:T(2,128)(2,1)} fusion(bf16[128,2,8192]{2,1,0:T(2,128)(2,1)} %broadcast_in_dim.95, s32[64]{0:T(128)S(1)} %compare_select_fusion.21, bf16[64,2,8192]{2,1,0:T(2,128)(2,1)S(1)} %reshape.356), kind=kCustom, calls=%fused_computation.5 | custom fusion | bytes 6291712 | tf_op jit(solution)/shard_map/scatter | solution.py:50
  122.9 99.8 %all-to-all-done.2 = bf16[128,1,2,8192]{3,2,1,0:T(2,128)(2,1)} async-done(((bf16[128,1,2,8192]{3,2,1,0:T(2,128)(2,1)}), bf16[128,1,2,8192]{3,2,1,0:T(2,128)(2,1)}, u32[]{:S(2)}, u32[]{:S(2)}) %all-to-all-start.2) | async-done | bytes 4194336 | tf_op jit(solution)/shard_map/all_to_all | solution.py:63
  224.7 20.7 %scatter_fusion.3 = bf16[64,2,8192]{2,1,0:T(2,128)(2,1)S(1)} fusion(bf16[64,2,8192]{2,1,0:T(2,128)(2,1)S(1)} %broadcast_in_dim.94, s32[128]{0:T(128)S(1)} %get-tuple-element.300, bf16[128,2,8192]{2,1,0:T(2,128)(2,1)} %bitcast.7), kind=kCustom, calls=%fused_computation.6 | custom fusion | bytes 12583424 | tf_op jit(solution)/shard_map/scatter | solution.py:97
  251.2 44.4 %all-gather.5.cloned.1.call-done = bf16[4096,1024]{1,0:T(8,128)(2,1)} async-done(((bf16[128,1024]{1,0:T(8,128)(2,1)}), bf16[4096,1024]{1,0:T(8,128)(2,1)}) %all-gather.5.cloned.1.call-update) | async-done | bytes 8388624 | tf_op jit(solution)/shard_map/all_gather | solution.py:145
  295.6 193.7 %all-gather.3.cloned.1.call-done = bf16[4096,1024]{1,0:T(8,128)(2,1)} async-done(((bf16[128,1024]{1,0:T(8,128)(2,1)}), bf16[4096,1024]{1,0:T(8,128)(2,1)}) %all-gather.3.cloned.1.call-update) | async-done | bytes 8388624 | tf_op jit(solution)/shard_map/all_gather | solution.py:144
  489.3 470.0 %while.18 = (s32[]{:T(128)}, f32[8,8,128]{2,1,0:T(8,128)S(1)}, f32[8,8,128]{2,1,0:T(8,128)S(1)}, f32[8,8,128,128]{3,2,1,0:T(8,128)}, s32[32]{0:T(128)S(1)}, /*in...) while((s32[]{:T(128)}, f32[8,8,128]{2,1,0:T(8,128)S(1)}, ...), condition=%wide.region_13.14_spmd.clone, body=%wide.region_10.13_spmd.clone.sunk | while | flops 551657472 | bytes 26282648 | solution.py:156
  556.2 5.9 fusion.52
  570.9 5.9 fusion.52
  600.3 5.9 fusion.52
  615.0 5.9 fusion.52
  629.7 5.9 fusion.52
  673.9 5.9 fusion.52
  718.0 5.9 fusion.52
  732.7 5.9 fusion.52
  967.4 11.8 %gather_fusion = bf16[128,2,8192]{2,1,0:T(2,128)(2,1)} fusion(bf16[64,2,8192]{2,1,0:T(2,128)(2,1)S(1)} %convert_element_type.46, s32[1024]{0:T(1024)S(1)} %pad_clamp_fusion.1), kind=kCustom, calls=%fused_computation | custom fusion | bytes 8389120 | tf_op jit(solution)/shard_map/gather | solution.py:165
  979.1 6.6 all-to-all-start.4
  985.8 53.2 %all-to-all-done.4 = bf16[128,1,2,8192]{3,2,1,0:T(2,128)(2,1)} async-done(((bf16[128,1,2,8192]{3,2,1,0:T(2,128)(2,1)}), bf16[128,1,2,8192]{3,2,1,0:T(2,128)(2,1)}, u32[]{:S(2)}, u32[]{:S(2)}) %all-to-all-start.4) | async-done | bytes 4194336 | tf_op jit(solution)/shard_map/all_to_all | solution.py:166
  1038.9 8.4 gather_fusion.1
  (425 shorter events, 470.8 us)
Async XLA Ops:
  6.5 115.8 %copy-start = (s32[4,2]{0,1:T(2,128)S(1)}, s32[4,2]{0,1:T(2,128)}, u32[]{:S(2)}) copy-start(s32[4,2]{0,1:T(2,128)} %param.13) | copy-start | bytes 100
  6.5 53.9 %copy-start.2 = (bf16[128,1024]{1,0:T(8,128)(2,1)S(1)}, bf16[128,1024]{1,0:T(8,128)(2,1)}, u32[]{:S(2)}) copy-start(bf16[128,1024]{1,0:T(8,128)(2,1)} %param.9) | copy-start | bytes 786436
  9.8 21.5 %all-to-all-start = ((bf16[128,1,1]{2,1,0:T(2,128)(2,1)}), bf16[128,1,1]{2,1,0:T(2,128)(2,1)S(1)}, u32[]{:S(2)}, u32[]{:S(2)}) async-start(bf16[128,1,1]{2,1,0:T(2,128)(2,1)} %copy.43), calls=%async_computation | async-start | bytes 131072 | tf_op jit(solution)/shard_map/all_to_all | solution.py:84
  31.4 23.5 %all-to-all-start.3 = ((bf16[128,1,2,1024]{3,2,1,0:T(2,128)(2,1)}), bf16[128,1,2,1024]{3,2,1,0:T(2,128)(2,1)S(1)}, u32[]{:S(2)}, u32[]{:S(2)}) async-start(bf16[128,1,2,1024]{3,2,1,0:T(2,128)(2,1)} %bitcast.9), calls=%async_computation.3 | async-start | bytes 1048576 | tf_op jit(solution)/shard_map/all_to_all | solution.py:77
  41.1 254.4 %all-gather.5.cloned.1.call-start = ((), (), s32[]{:S(2)}) async-start(), calls=%async_computation.6 | async-start | bytes 8650752 | tf_op jit(solution)/shard_map/all_gather | solution.py:145
  60.3 428.9 %all-gather.3.cloned.1.call-start = ((), (), s32[]{:S(2)}) async-start(), calls=%async_computation.5 | async-start | bytes 8650752 | tf_op jit(solution)/shard_map/all_gather | solution.py:144
  116.6 106.1 %all-to-all-start.2 = ((bf16[128,1,2,8192]{3,2,1,0:T(2,128)(2,1)}), bf16[128,1,2,8192]{3,2,1,0:T(2,128)(2,1)}, u32[]{:S(2)}, u32[]{:S(2)}) async-start(bf16[128,1,2,8192]{3,2,1,0:T(2,128)(2,1)} %bitcast.78), calls=%async_computation.2 | async-start | bytes 8388608 | tf_op jit(solution)/shard_map/all_to_all | solution.py:63
  979.1 59.8 %all-to-all-start.4 = ((bf16[128,1,2,8192]{3,2,1,0:T(2,128)(2,1)}), bf16[128,1,2,8192]{3,2,1,0:T(2,128)(2,1)}, u32[]{:S(2)}, u32[]{:S(2)}) async-start(bf16[128,1,2,8192]{3,2,1,0:T(2,128)(2,1)} %bitcast.79), calls=%async_computation.4 | async-start | bytes 8388608 | tf_op jit(solution)/shard_map/all_to_all | solution.py:166
  1038.9 10.6 %copy-start.1 = (s32[4,2]{0,1:T(2,128)S(1)}, s32[4,2]{0,1:T(2,128)}, u32[]{:S(2)}) copy-start(s32[4,2]{0,1:T(2,128)} %param.13) | copy-start | bytes 100
Sparse Core Ops, SparseCore 0:
  60.5 235.0 all-gather.4
  297.2 192.0 all-gather.2
where the time goes:
time: 1060 us
  waiting for transfers between devices  402 us (38%)
  matrix products  277 us (26%)
  local copies, waits for them, and re-layouts  169 us (16%)
  other arithmetic  135 us (13%)
  starting transfers between devices  33.7 us (3%)
  blocking collectives  23.9 us (2%)
  between operations  13.6 us (1%)
    all_gather x1, waiting for transfers between devices, shards(): key_piece = lax.all_gather(local_key, 'seq', axis=0, tiled=True)  194 us
    dot_general x32, matrix products, attend(): jnp.einsum('hgqk,khd->hgqd', weights.astype(jnp.bfloat16), value_heads, p...  187 us
    reduce_sum x32, other arithmetic, attend(): totals = totals * rescale + jnp.sum(weights, axis=-1)  103 us
    all_to_all x1, waiting for transfers between devices, shards(): lax.all_to_all(send_query.reshape(devices, capacity, block_rows, query_wi...  99.8 us
    dot_general x32, matrix products, attend(): jnp.einsum('qhgd,khd->hgqk', query_heads, key_heads, preferred_element_ty...  90 us
    dynamic_slice x128, local copies, waits for them, and re-layouts, shards(): running, unused = lax.scan(scan_step, running, (keyed, valued, offsets))  63.7 us
    all_to_all x1, waiting for transfers between devices, shards(): lax.all_to_all(returning.reshape(devices, capacity, block_rows, query_wid...  53.2 us
    all_gather x1, waiting for transfers between devices, shards(): value_piece = lax.all_gather(local_value, 'seq', axis=0, tiled=True)  44.4 us
  transfers between devices with their start and end apart: 6, of which 5 were waited for; matrix products, arithmetic and copies ran while one was open for 7% of the time, Pallas kernels for 0%

commit v1 on v0

--- a/solution.py
+++ b/solution.py
@@ -141,7 +141,10 @@
         jnp.zeros((KEY_HEADS, groups, row_count, HEAD_SIZE), jnp.float32),
     )
     running = initial
-    key_piece = lax.all_gather(local_key, "seq", axis=0, tiled=True)
+    count = lax.axis_size("seq")
+    pieces = jnp.stack([local_key for _ in range(count)])
+    pieces = lax.all_to_all(pieces, "seq", split_axis=0, concat_axis=0)
+    key_piece = jnp.concatenate(pieces, axis=0)
     value_piece = lax.all_gather(local_value, "seq", axis=0, tiled=True)
     piece_rows = key_piece.shape[0]
     shard_count = piece_rows // row_count

time: 1060 us -> 1020 us (0.962)
  waiting for transfers between devices: 402 us -> 338 us
  local copies, waits for them, and re-layouts: 169 us -> 203 us
  blocking collectives: 23.9 us -> 0 us
  starting transfers between devices: 33.7 us -> 47.2 us
    all_gather x1 -> x0, waiting for transfers between devices: 194 us -> none  [shards(): key_piece = lax.all_gather(local_key, 'seq', axis=0, tiled=True)]
    all_to_all x0 -> x2, waiting for transfers between devices: none -> 178 us  [the longest x1 178 us: shards(): pieces = lax.all_to_all(pieces, 'seq', split_axis=0, concat_axis=0)]
    all_gather x1, waiting for transfers between devices: 44.4 us -> 0.01 us  [shards(): value_piece = lax.all_gather(local_value, 'seq', axis=0, tiled=True)]
    all_to_all x1 -> x0, blocking collectives: 23.9 us -> none  [shards(): lax.all_to_all(send_key.reshape(devices, capacity, block_rows, key_width)...]
    dynamic_slice x128, local copies, waits for them, and re-layouts: 63.7 us -> 86.4 us  [shards(): running, unused = lax.scan(scan_step, running, (keyed, valued, offsets))]
  transfers between devices with their start and end apart: 6 -> 7, of which waited for: 5 -> 4; matrix products, arithmetic and copies ran while one was open for 7% -> 8% of each run, Pallas kernels for 0% -> 0%
where the time goes in v1:
time: 1020 us; the launch traced here: 1010 us
  waiting for transfers between devices  338 us (33%)
  matrix products  276 us (27%)
  local copies, waits for them, and re-layouts  203 us (20%)
  other arithmetic  135 us (13%)
  starting transfers between devices  47.2 us (5%)
  between operations  13.6 us (1%)
    dot_general x32, matrix products, attend(): jnp.einsum('hgqk,khd->hgqd', weights.astype(jnp.bfloat16), value_heads, p...  187 us
    all_to_all x1, waiting for transfers between devices, shards(): pieces = lax.all_to_all(pieces, 'seq', split_axis=0, concat_axis=0)  178 us
    reduce_sum x32, other arithmetic, attend(): totals = totals * rescale + jnp.sum(weights, axis=-1)  103 us
    all_to_all x1, waiting for transfers between devices, shards(): lax.all_to_all(send_query.reshape(devices, capacity, block_rows, query_wi...  95.5 us
    dot_general x32, matrix products, attend(): jnp.einsum('qhgd,khd->hgqk', query_heads, key_heads, preferred_element_ty...  88.6 us
    dynamic_slice x128, local copies, waits for them, and re-layouts, shards(): running, unused = lax.scan(scan_step, running, (keyed, valued, offsets))  86.4 us
    all_to_all x1, waiting for transfers between devices, shards(): lax.all_to_all(returning.reshape(devices, capacity, block_rows, query_wid...  53.2 us
    scatter x3, local copies, waits for them, and re-layouts, pack_rows(): empty.at[destination].set(payload.reshape(blocks, block_rows, width))  30.5 us
  transfers between devices with their start and end apart: 7, of which 4 were waited for; matrix products, arithmetic and copies ran while one was open for 8% of the time, Pallas kernels for 0%

profile of v1, /device:TPU:1, one launch (start us, length us, event | category | flops | bytes accessed | tf_op | source)
XLA Modules:
  0.0 1013.0 jit_solution(8319132077649285125)
XLA Ops:
  9.8 11.5 %all-to-all-start = ((bf16[128,1,1]{2,1,0:T(2,128)(2,1)}), bf16[128,1,1]{2,1,0:T(2,128)(2,1)S(1)}, u32[]{:S(2)}, u32[]{:S(2)}) async-start(bf16[128,1,1]{2,1,0:T(2,128)(2,1)} %copy.45), calls=%async_computation | async-start | bytes 131072 | tf_op jit(solution)/shard_map/all_to_all | solution.py:84
  23.5 7.9 scatter_fusion.4
  31.4 9.8 all-to-all-start.4
  43.6 11.3 %all-to-all-done.4 = bf16[128,1,2,1024]{3,2,1,0:T(2,128)(2,1)S(1)} async-done(((bf16[128,1,2,1024]{3,2,1,0:T(2,128)(2,1)}), bf16[128,1,2,1024]{3,2,1,0:T(2,128)(2,1)S(1)}, u32[]{:S(2)}, u32[]{:S(2)}) %all-to-all-start.4) | async-done | bytes 524320 | tf_op jit(solution)/shard_map/all_to_all | solution.py:77
  61.5 7.9 scatter_fusion
  77.1 6.2 broadcast_in_dim.95
  83.3 14.6 %scatter_fusion.2 = bf16[128,2,8192]{2,1,0:T(2,128)(2,1)} fusion(bf16[128,2,8192]{2,1,0:T(2,128)(2,1)} %broadcast_in_dim.95, s32[64]{0:T(128)S(1)} %compare_select_fusion.21, bf16[64,2,8192]{2,1,0:T(2,128)(2,1)S(1)} %reshape.350), kind=kCustom, calls=%fused_computation.5 | custom fusion | bytes 6291712 | tf_op jit(solution)/shard_map/scatter | solution.py:50
  97.9 10.4 %all-to-all-start.3 = ((bf16[128,1,2,8192]{3,2,1,0:T(2,128)(2,1)}), bf16[128,1,2,8192]{3,2,1,0:T(2,128)(2,1)}, u32[]{:S(2)}, u32[]{:S(2)}) async-start(bf16[128,1,2,8192]{3,2,1,0:T(2,128)(2,1)} %bitcast.79), calls=%async_computation.3 | async-start | bytes 8388608 | tf_op jit(solution)/shard_map/all_to_all | solution.py:63
  113.2 95.5 %all-to-all-done.3 = bf16[128,1,2,8192]{3,2,1,0:T(2,128)(2,1)} async-done(((bf16[128,1,2,8192]{3,2,1,0:T(2,128)(2,1)}), bf16[128,1,2,8192]{3,2,1,0:T(2,128)(2,1)}, u32[]{:S(2)}, u32[]{:S(2)}) %all-to-all-start.3) | async-done | bytes 4194336 | tf_op jit(solution)/shard_map/all_to_all | solution.py:63
  221.4 20.7 %scatter_fusion.3 = bf16[64,2,8192]{2,1,0:T(2,128)(2,1)S(1)} fusion(bf16[64,2,8192]{2,1,0:T(2,128)(2,1)S(1)} %broadcast_in_dim.94, s32[128]{0:T(128)S(1)} %get-tuple-element.298, bf16[128,2,8192]{2,1,0:T(2,128)(2,1)} %bitcast.7), kind=kCustom, calls=%fused_computation.6 | custom fusion | bytes 12583424 | tf_op jit(solution)/shard_map/scatter | solution.py:97
  247.8 177.5 %all-to-all-done.2 = bf16[32,128,1024]{1,2,0:T(8,128)(2,1)} async-done(((bf16[32,128,1024]{1,2,0:T(8,128)(2,1)}), bf16[32,128,1024]{1,2,0:T(8,128)(2,1)}, u32[]{:S(2)}, u32[]{:S(2)}) %all-to-all-start.2) | async-done | bytes 8388640 | tf_op jit(solution)/shard_map/all_to_all | solution.py:146
  425.4 491.2 %while.18 = (s32[]{:T(128)}, f32[8,8,128]{2,1,0:T(8,128)S(1)}, f32[8,8,128]{2,1,0:T(8,128)S(1)}, f32[8,8,128,128]{3,2,1,0:T(8,128)}, s32[32]{0:T(128)S(1)}, /*in...) while((s32[]{:T(128)}, f32[8,8,128]{2,1,0:T(8,128)S(1)}, ...), condition=%wide.region_13.14_spmd.clone, body=%wide.region_10.13_spmd.clone.sunk | while | flops 551657472 | bytes 25758364 | solution.py:159
  464.8 5.9 fusion.52
  510.9 5.9 fusion.52
  526.3 5.9 fusion.52
  557.1 5.9 fusion.52
  572.4 5.9 fusion.52
  603.2 5.9 fusion.52
  649.3 5.9 fusion.52
  664.7 5.9 fusion.52
  924.6 11.8 %gather_fusion = bf16[128,2,8192]{2,1,0:T(2,128)(2,1)} fusion(bf16[64,2,8192]{2,1,0:T(2,128)(2,1)S(1)} %convert_element_type.46, s32[1024]{0:T(1024)S(1)} %pad_clamp_fusion.1), kind=kCustom, calls=%fused_computation | custom fusion | bytes 8389120 | tf_op jit(solution)/shard_map/gather | solution.py:168
  936.4 6.0 all-to-all-start.5
  942.4 53.2 %all-to-all-done.5 = bf16[128,1,2,8192]{3,2,1,0:T(2,128)(2,1)} async-done(((bf16[128,1,2,8192]{3,2,1,0:T(2,128)(2,1)}), bf16[128,1,2,8192]{3,2,1,0:T(2,128)(2,1)}, u32[]{:S(2)}, u32[]{:S(2)}) %all-to-all-start.5) | async-done | bytes 4194336 | tf_op jit(solution)/shard_map/all_to_all | solution.py:169
  995.6 8.4 gather_fusion.1
  (427 shorter events, 498.6 us)
Async XLA Ops:
  6.5 212.3 %copy-start = (s32[4,2]{0,1:T(2,128)S(1)}, s32[4,2]{0,1:T(2,128)}, u32[]{:S(2)}) copy-start(s32[4,2]{0,1:T(2,128)} %param.13) | copy-start | bytes 100
  6.5 53.8 %copy-start.2 = (bf16[128,1024]{1,0:T(8,128)(2,1)S(1)}, bf16[128,1024]{1,0:T(8,128)(2,1)}, u32[]{:S(2)}) copy-start(bf16[128,1024]{1,0:T(8,128)(2,1)} %param.9) | copy-start | bytes 786436
  9.8 21.5 %all-to-all-start = ((bf16[128,1,1]{2,1,0:T(2,128)(2,1)}), bf16[128,1,1]{2,1,0:T(2,128)(2,1)S(1)}, u32[]{:S(2)}, u32[]{:S(2)}) async-start(bf16[128,1,1]{2,1,0:T(2,128)(2,1)} %copy.45), calls=%async_computation | async-start | bytes 131072 | tf_op jit(solution)/shard_map/all_to_all | solution.py:84
  31.4 23.5 %all-to-all-start.4 = ((bf16[128,1,2,1024]{3,2,1,0:T(2,128)(2,1)}), bf16[128,1,2,1024]{3,2,1,0:T(2,128)(2,1)S(1)}, u32[]{:S(2)}, u32[]{:S(2)}) async-start(bf16[128,1,2,1024]{3,2,1,0:T(2,128)(2,1)} %bitcast.9), calls=%async_computation.4 | async-start | bytes 1048576 | tf_op jit(solution)/shard_map/all_to_all | solution.py:77
  41.1 384.2 %all-gather.2.cloned.1.call-start = ((), (), s32[]{:S(2)}) async-start(), calls=%async_computation.6 | async-start | bytes 8650752 | tf_op jit(solution)/shard_map/all_gather | solution.py:148
  69.4 28.5 %all-to-all-start.1 = ((bf16[128,1,2,1024]{3,2,1,0:T(2,128)(2,1)}), bf16[128,1,2,1024]{3,2,1,0:T(2,128)(2,1)S(1)}, u32[]{:S(2)}, u32[]{:S(2)}) async-start(bf16[128,1,2,1024]{3,2,1,0:T(2,128)(2,1)} %bitcast.4), calls=%async_computation.1 | async-start | bytes 1048576 | tf_op jit(solution)/shard_map/all_to_all | solution.py:70
  97.9 110.9 %all-to-all-start.3 = ((bf16[128,1,2,8192]{3,2,1,0:T(2,128)(2,1)}), bf16[128,1,2,8192]{3,2,1,0:T(2,128)(2,1)}, u32[]{:S(2)}, u32[]{:S(2)}) async-start(bf16[128,1,2,8192]{3,2,1,0:T(2,128)(2,1)} %bitcast.79), calls=%async_computation.3 | async-start | bytes 8388608 | tf_op jit(solution)/shard_map/all_to_all | solution.py:63
  213.9 211.5 %all-to-all-start.2 = ((bf16[32,128,1024]{1,2,0:T(8,128)(2,1)}), bf16[32,128,1024]{1,2,0:T(8,128)(2,1)}, u32[]{:S(2)}, u32[]{:S(2)}) async-start(bf16[32,128,1024]{1,2,0:T(8,128)(2,1)} %stack.3), calls=%async_computation.2 | async-start | bytes 16777216 | tf_op jit(solution)/shard_map/all_to_all | solution.py:146
  936.4 59.2 %all-to-all-start.5 = ((bf16[128,1,2,8192]{3,2,1,0:T(2,128)(2,1)}), bf16[128,1,2,8192]{3,2,1,0:T(2,128)(2,1)}, u32[]{:S(2)}, u32[]{:S(2)}) async-start(bf16[128,1,2,8192]{3,2,1,0:T(2,128)(2,1)} %bitcast.80), calls=%async_computation.5 | async-start | bytes 8388608 | tf_op jit(solution)/shard_map/all_to_all | solution.py:169
  995.6 10.6 %copy-start.1 = (s32[4,2]{0,1:T(2,128)S(1)}, s32[4,2]{0,1:T(2,128)}, u32[]{:S(2)}) copy-start(s32[4,2]{0,1:T(2,128)} %param.13) | copy-start | bytes 100
Sparse Core Ops, SparseCore 0:
  60.4 337.4 all-gather.1
